TPU v7x, 128 devices: a whole 4x4x4 slice. The times are simulated.
128 devices in a mesh: segment: 2 (over z_hi), dp: 32 (over y, x, core), rows: 2 (over z_lo).
Axes of the slice: x: 4, y: 4, z: 4 (z_hi: 2, z_lo: 2; z = z_hi * 2 + z_lo), core: 2. Of those that a mesh axis runs over, the one named last changes fastest.
Arguments:
- segment_inputs: bfloat16 [2, 64, 32, 32, 640], P('segment', 'dp', 'rows'), may hold values from -6 to 6
- weights: bfloat16 [2, 9, 640, 640], P('segment', None, 'dp'), may hold values from -0.078125 to 0.078125
- gains: float32 [2, 640], P('segment'), may hold values from 0.5 to 1.5
- shifts: float32 [2, 640], P('segment'), may hold values from -3 to 3
- chain_cot: bfloat16 [64, 32, 32, 640], P('dp', 'rows'), may hold values from -6 to 6
- skip_cot: bfloat16 [64, 32, 32, 640], P('dp', 'rows'), may hold values from -6 to 6
Outputs:
- input_grads: bfloat16 [2, 64, 32, 32, 640], P('segment', 'dp', 'rows')
- weight_grads: float32 [2, 9, 640, 640], P('segment', None, 'dp')
- gain_grads: float32 [2, 640], P('segment')
- shift_grads: float32 [2, 640], P('segment')
All inputs are finite; a program needn't handle non-finite values.
Results may differ from a plain program's by a relative error of at most 0.0014.
The roundings to bfloat16 on the way count: a program that leaves them out, or rounds other values in their place, can miss the bound.
Values may be sent and summed in bfloat16 or wider, within the bound.
No kernel may reach another device: no remote copies, remote signals or barrier semaphores. Data moves between devices by JAX's collectives and lax.ppermute only.
A program may use at most 128 MiB of HBM per device.

v0:
```python
import jax
import jax.numpy as jnp
from jax import lax
from jax.sharding import PartitionSpec as P

GROUPS = 16


epsilon = 1e-05
offsets = [(-1, -1), (-1, 0), (-1, 1), (0, -1), (0, 0), (0, 1), (1, -1), (1, 0), (1, 1)]


def extended(shard, sides, width):
    for axis, dim in sides:
        count, length = (lax.axis_size(axis), shard.shape[dim])
        up = [(i, (i + 1) % count) for i in range(count - 1)]
        down = [(j, i) for i, j in up]
        last = lax.slice_in_dim(shard, length - width, length, axis=dim)
        first = lax.slice_in_dim(shard, 0, width, axis=dim)
        before = lax.ppermute(last, axis, up)
        after = lax.ppermute(first, axis, down)
        shard = jnp.concatenate([before, shard, after], axis=dim)
    return shard


def shifted_2(shard, axis, by):
    count = lax.axis_size(axis)
    pairs = [(i, i + by) for i in range(count) if 0 <= i + by < count]
    return lax.ppermute(shard, axis, pairs)


def stencil(padded, height, columns):
    return jnp.stack(
        [
            padded[1 - row_off : 1 - row_off + height, 1 - col_off : 1 - col_off + columns]
            for row_off, col_off in offsets
        ],
        axis=2,
    )


def project(shifted, piece_rows):
    return jnp.einsum("pko,kio->pi", shifted, piece_rows, preferred_element_type=jnp.float32)


def shards(segment_inputs, weights, gains, shifts, chain_cot, skip_cot):
    micro_count = segment_inputs.shape[1]
    height, columns, channels = segment_inputs.shape[2:]
    per_group = channels // GROUPS
    pixels = height * columns
    count_all = float(height * lax.axis_size("rows") * columns * per_group)
    segment_pos = lax.axis_index("segment")
    weight_local = weights[0]
    gain = gains[0]
    shift = shifts[0]
    local_inputs = segment_inputs[0]
    weight_grad = jnp.zeros((channels, 9, channels), jnp.float32)
    gain_grad = jnp.zeros((channels,), jnp.float32)
    shift_grad = jnp.zeros((channels,), jnp.float32)
    received = jnp.zeros((height, columns, channels), jnp.bfloat16)
    outputs = jnp.zeros_like(local_inputs)
    for moment in range(micro_count + 1):
        sample = moment - 1 + segment_pos
        in_range = (sample >= 0) & (sample < micro_count)
        clipped = jnp.clip(sample, 0, micro_count - 1)
        inputs = lax.dynamic_index_in_dim(local_inputs, clipped, 0, keepdims=False).astype(
            jnp.float32
        )
        chain_one = lax.dynamic_index_in_dim(chain_cot, clipped, 0, keepdims=False)
        skip_one = lax.dynamic_index_in_dim(skip_cot, clipped, 0, keepdims=False)
        outside = chain_one.astype(jnp.float32) + skip_one.astype(jnp.float32)
        adjoint = jnp.where(segment_pos == 1, outside.astype(jnp.bfloat16), received)
        adjoint = jnp.where(in_range, adjoint, jnp.zeros_like(adjoint))
        grouped = inputs.reshape(pixels, GROUPS, per_group)
        group_sums, squares = lax.psum(
            (jnp.sum(grouped, axis=(0, 2)), jnp.sum(grouped * grouped, axis=(0, 2))), "rows"
        )
        group_mean = group_sums / count_all
        inv_std = lax.rsqrt(squares / count_all - group_mean * group_mean + epsilon)
        normed = ((grouped - group_mean[None, :, None]) * inv_std[None, :, None]).reshape(
            pixels, channels
        )
        preact = normed * gain + shift
        gate_val = jax.nn.sigmoid(preact)
        active = (preact * gate_val).astype(jnp.bfloat16)
        padded = extended(adjoint, (("rows", 0),), 1)
        padded = jnp.pad(padded, ((0, 0), (1, 1), (0, 0)))
        shifted = stencil(padded, height, columns).reshape(pixels, 9, channels)
        back_prop = project(shifted, lax.all_gather(weight_local, "dp", axis=1, tiled=True))
        weight_grad = weight_grad + jnp.einsum(
            "pi,pko->iko", active, shifted, preferred_element_type=jnp.float32
        )
        pre_grad = back_prop * (gate_val * (1.0 + preact * (1.0 - gate_val)))
        gain_grad = gain_grad + jnp.sum(pre_grad * normed, axis=0)
        shift_grad = shift_grad + jnp.sum(pre_grad, axis=0)
        norm_grad = (pre_grad * gain).reshape(pixels, GROUPS, per_group)
        norm_group = normed.reshape(pixels, GROUPS, per_group)
        first_sum, second = lax.psum(
            (jnp.sum(norm_grad, axis=(0, 2)), jnp.sum(norm_grad * norm_group, axis=(0, 2))), "rows"
        )
        first_mean = first_sum / count_all
        second_mean = second / count_all
        in_grad = (
            inv_std[None, :, None]
            * (norm_grad - first_mean[None, :, None] - norm_group * second_mean[None, :, None])
        ).reshape(height, columns, channels)
        handed = in_grad.astype(jnp.bfloat16)
        result = jnp.where(segment_pos == 0, (outside + in_grad).astype(jnp.bfloat16), handed)
        current = lax.dynamic_index_in_dim(outputs, clipped, 0, keepdims=False)
        outputs = lax.dynamic_update_index_in_dim(
            outputs, jnp.where(in_range, result, current), clipped, 0
        )
        if moment < micro_count:
            received = shifted_2(handed, "segment", -1)
    weight_shard = lax.psum_scatter(weight_grad, "dp", scatter_dimension=0, tiled=True)
    weight_shard = lax.psum(weight_shard, "rows")
    gain_grad, shift_grad = lax.psum((gain_grad, shift_grad), ("dp", "rows"))
    return (
        outputs[None],
        jnp.transpose(weight_shard, (1, 0, 2))[None],
        gain_grad[None],
        shift_grad[None],
    )


def solution(mesh):
    placed = (
        P("segment", "dp", "rows", None, None),
        P("segment", None, "dp", None),
        P("segment", None),
        P("segment", None),
        P("dp", "rows", None, None),
        P("dp", "rows", None, None),
    )
    return jax.shard_map(
        shards,
        mesh=mesh,
        in_specs=placed,
        out_specs=(
            P("segment", "dp", "rows", None, None),
            P("segment", None, "dp", None),
            P("segment", None),
            P("segment", None),
        ),
        check_vma=False,
    )
```

profile of v0, /device:TPU:0, one launch (start us, length us, event | category | flops | bytes accessed | tf_op | source)
XLA Modules:
  0.0 505.6 jit_solution(16634968469487333070)
XLA Ops:
  10.7 3.9 collective-permute-start
  16.9 5.5 %all-reduce.8 = (f32[16]{0:T(128)S(1)}, f32[16]{0:T(128)S(1)}) all-reduce(f32[16]{0:T(128)S(1)} %reduce_sum.194, f32[16]{0:T(128)S(1)} %reduce_sum.200), channel_id=1, replica_groups=mesh['segment'=2,'dp'=32,'rows'=2] {'rows'}, use_global_device_ids=true, to_apply=%region_2.3 | all-reduce | flops 32 | bytes 256 | tf_op jit(solution)/shard_map/psum | solution.py:75
  34.0 43.2 %all-gather.3.cloned.1.call-done = bf16[1,9,640,640]{3,1,0,2:T(8,128)(2,1)} async-done(((bf16[1,9,20,640]{3,1,0,2:T(8,128)(2,1)}), bf16[1,9,640,640]{3,1,0,2:T(8,128)(2,1)}) %all-gather.3.cloned.1.call-update) | async-done | bytes 7372816 | tf_op jit(solution)/shard_map/all_gather | solution.py:89
  77.2 12.0 %multiply_reduce_fusion.2 = (f32[640]{0:T(1024)S(1)}, f32[640]{0:T(1024)S(1)}, f32[640]{0:T(1024)S(1)}, f32[640]{0:T(1024)S(1)}, f32[512,640]{1,0:T(8,128)S(1)}) fusion(f32[640]{0:T(1024)S(1)} %mul.348, f32[640]{0:T(1024)S(1)} %sub.238, bf16[1,2,16,32,640]{4,3,2,1,0:T(8,128)(2,1)S(1)} %copy-done, s32[]{:T(128)S(6)} %min.10, f32[640]{0:T(1024)S(1)} %reduce.24, ...), kind=kOutput, calls=%fused_computation.51 | convolution fusion | flops 3780769792 | bytes 16565764 | tf_op jit(solution)/shard_map/pko,kio->pi/dot_general | solution.py:43
  89.7 4.9 all-reduce.7
  97.8 12.1 %fusion.74 = f32[640,9,640]{2,0,1:T(8,128)} fusion(bf16[512,9,640]{2,0,1:T(8,128)(2,1)} %constant_dynamic-update-slice_fusion, f32[512,640]{1,0:T(8,128)S(1)} %copy-done.9), kind=kOutput, calls=%fused_computation.112 | convolution fusion | flops 3776512000 | bytes 21954560 | tf_op jit(solution)/shard_map/pi,pko->iko/dot_general | solution.py:90
  110.2 5.5 %collective-permute-done.2 = bf16[16,32,640]{2,1,0:T(8,128)(2,1)S(1)} collective-permute-done((bf16[16,32,640]{2,1,0:T(8,128)(2,1)}, bf16[16,32,640]{2,1,0:T(8,128)(2,1)S(1)}, u32[]{:S(2)}, u32[]{:S(2)}) %collective-permute-start.2) | collective-permute-done | bytes 655392 | tf_op jit(solution)/shard_map/ppermute | solution.py:29
  117.0 3.5 collective-permute-start.3
  122.2 4.2 collective-permute-done.4
  128.2 13.3 %multiply_reduce_fusion.1 = (f32[640]{0:T(1024)S(1)}, f32[640]{0:T(1024)S(1)}, f32[640]{0:T(1024)S(1)}, f32[640]{0:T(1024)S(1)}, f32[512,640]{1,0:T(8,128)}) fusion(f32[640]{0:T(1024)S(1)} %mul.369, f32[640]{0:T(1024)S(1)} %sub.256, bf16[1,2,16,32,640]{4,3,2,1,0:T(8,128)(2,1)S(1)} %copy-done, s32[]{:T(128)S(6)} %min.11, f32[640]{0:T(1024)S(1)} %reduce.24, ...), kind=kOutput, calls=%fused_computation.50 | convolution fusion | flops 3780769792 | bytes 16565764 | tf_op jit(solution)/shard_map/pko,kio->pi/dot_general | solution.py:43
  141.9 5.2 %all-reduce.6 = (f32[16]{0:T(128)S(1)}, f32[16]{0:T(128)S(1)}, f32[16]{0:T(128)S(1)}, f32[16]{0:T(128)S(1)}) all-reduce(f32[16]{0:T(128)S(1)} %reduce_sum.269, f32[16]{0:T(128)S(1)} %reduce_sum.266, f32[16]{0:T(128)S(1)} %reduce_sum.272, f32[16]{0:T(128)S(1)} %reduce_sum.275), channel_id=1, replica_groups=mesh['segment'=2,'dp'=32,'rows'=2] {'rows'}, use_global_device_ids=true, to_apply=%region_23.24 | all-reduce | flops 64 | bytes 512 | tf_op jit(solution)/shard_map/psum | solution.py:98
  147.4 2.5 fusion.34
  151.6 12.5 %fusion.72 = f32[640,9,640]{2,0,1:T(8,128)} fusion(bf16[512,9,640]{2,0,1:T(8,128)(2,1)} %copy-done.11, f32[512,640]{1,0:T(8,128)} %copy-done.10), kind=kOutput, calls=%fused_computation.110 | convolution fusion | flops 3776512000 | bytes 21954560 | tf_op jit(solution)/shard_map/pi,pko->iko/dot_general | solution.py:90
  166.1 2.2 collective-permute-start.6
  169.9 4.2 collective-permute-done.7
  183.2 20.8 %add_add_fusion = f32[640,9,640]{2,0,1:T(8,128)} fusion(f32[640,9,640]{2,0,1:T(8,128)} %fusion.74, f32[640,9,640]{2,0,1:T(8,128)} %fusion.72, bf16[512,9,640]{2,0,1:T(8,128)(2,1)} %constant_dynamic-update-slice_fusion.18, f32[512,640]{1,0:T(8,128)S(1)} %fusion.29, f32[640]{0:T(1024)S(1)} %reduce.25, f32[640]{0:T(1024)S(1)} %reduce.24), kind=kOutput, calls=%fused_computation | convolution fusion | flops 3784540160 | bytes 51450880 | tf_op jit(solution)/shard_map/pi,pko->iko/dot_general | solution.py:90
  206.1 2.5 fusion.63
  211.4 13.8 %multiply_reduce_fusion = (f32[640]{0:T(1024)S(1)}, f32[640]{0:T(1024)S(1)}, f32[640]{0:T(1024)S(1)}, f32[640]{0:T(1024)S(1)}, f32[512,640]{1,0:T(8,128)}) fusion(f32[640]{0:T(1024)S(1)} %mul.393, f32[640]{0:T(1024)S(1)} %sub.274, bf16[1,2,16,32,640]{4,3,2,1,0:T(8,128)(2,1)S(1)} %copy-done, s32[]{:T(128)S(6)} %min.12, f32[640]{0:T(1024)S(1)} %reduce.24, ...), kind=kOutput, calls=%fused_computation.49 | convolution fusion | flops 3781425152 | bytes 16568324 | tf_op jit(solution)/shard_map/pko,kio->pi/dot_general | solution.py:43
  225.6 4.9 all-reduce.5
  230.5 114.9 %all-reduce.14.cloned.1.call-done = f32[640,9,640]{2,0,1:T(8,128)} async-done(((f32[640,9,640]{2,0,1:T(8,128)}), f32[640,9,640]{2,0,1:T(8,128)}) %all-reduce.14.cloned.1.call-update) | async-done | bytes 14745616
  345.4 2.0 dynamic-slice_bitcast_fusion
  347.7 145.5 %all-reduce.4 = (f32[1,640]{1,0:T(1,128)}, f32[1,640]{1,0:T(1,128)}) all-reduce(f32[1,640]{1,0:T(1,128)S(1)} %broadcast_in_dim.20, f32[1,640]{1,0:T(1,128)S(1)} %broadcast_in_dim.21), channel_id=1, replica_groups=mesh['segment'=2,'dp'=32,'rows'=2] {'dp','rows'}, use_global_device_ids=true, to_apply=%region_41.42 | all-reduce | flops 1280 | bytes 10240 | tf_op jit(solution)/shard_map/psum | solution.py:117
  493.2 3.1 fusion.70
  496.3 2.3 copy.25
  (160 shorter events, 45.6 us)
Async XLA Ops:
  7.2 70.0 %all-gather.3.cloned.1.call-start = ((), (), s32[]{:S(2)}) async-start(), calls=%async_computation.1 | async-start | bytes 13516800 | tf_op jit(solution)/shard_map/all_gather | solution.py:89
  9.0 7.0 %copy-start = (bf16[1,2,16,32,640]{4,3,2,1,0:T(8,128)(2,1)S(1)}, bf16[1,2,16,32,640]{4,3,2,1,0:T(8,128)(2,1)}, u32[]{:S(2)}) copy-start(bf16[1,2,16,32,640]{4,3,2,1,0:T(8,128)(2,1)} %param.6) | copy-start | bytes 3932164
  9.0 336.4 %all-reduce.14.cloned.1.call-start = ((), (), s32[]{:S(2)}) async-start(), calls=%async_computation.2 | async-start | bytes 29491200
  10.7 12.1 %copy-start.12 = (f32[1,640]{1,0:T(1,128)S(1)}, f32[1,640]{1,0:T(1,128)}, u32[]{:S(2)}) copy-start(f32[1,640]{1,0:T(1,128)} %param.8) | copy-start | bytes 7684
  10.7 12.2 %copy-start.13 = (f32[1,640]{1,0:T(1,128)S(1)}, f32[1,640]{1,0:T(1,128)}, u32[]{:S(2)}) copy-start(f32[1,640]{1,0:T(1,128)} %param.9) | copy-start | bytes 7684
  10.7 14.3 %collective-permute-start = (bf16[1,32,640]{2,1,0:T(8,128)(2,1)S(1)}, bf16[1,32,640]{2,1,0:T(8,128)(2,1)S(1)}, u32[]{:S(2)}, u32[]{:S(2)}) collective-permute-start(bf16[1,32,640]{2,1,0:T(8,128)(2,1)S(1)} %get-tuple-element.79), channel_id=1, source_target_pairs={{0,1},{2,3},{4,5},{6,7},{8,9},{10,11},{12,13},{14,15},{16,17},{18,... | collective-permute-start | bytes 122888 | tf_op jit(solution)/shard_map/ppermute | solution.py:20
  14.7 10.3 %collective-permute-start.1 = (bf16[1,32,640]{2,1,0:T(8,128)(2,1)S(1)}, bf16[1,32,640]{2,1,0:T(8,128)(2,1)S(1)}, u32[]{:S(2)}, u32[]{:S(2)}) collective-permute-start(bf16[1,32,640]{2,1,0:T(8,128)(2,1)S(1)} %get-tuple-element.80), channel_id=1, source_target_pairs={{1,0},{3,2},{5,4},{7,6},{9,8},{11,10},{13,12},{15,14},{17,16},{19,... | collective-permute-start | bytes 122888 | tf_op jit(solution)/shard_map/ppermute | solution.py:21
  89.2 5.7 %copy-start.7 = (f32[512,640]{1,0:T(8,128)}, f32[512,640]{1,0:T(8,128)S(1)}, u32[]{:S(2)}) copy-start(f32[512,640]{1,0:T(8,128)S(1)} %get-tuple-element.50) | copy-start | bytes 3932164
  94.9 2.8 copy-start.9
  96.2 19.5 %copy-start.1 = (bf16[2,16,32,640]{3,2,1,0:T(8,128)(2,1)S(1)}, bf16[2,16,32,640]{3,2,1,0:T(8,128)(2,1)}, u32[]{:S(2)}) copy-start(bf16[2,16,32,640]{3,2,1,0:T(8,128)(2,1)} %param.11) | copy-start | bytes 3932164
  96.2 19.5 %collective-permute-start.2 = (bf16[16,32,640]{2,1,0:T(8,128)(2,1)}, bf16[16,32,640]{2,1,0:T(8,128)(2,1)S(1)}, u32[]{:S(2)}, u32[]{:S(2)}) collective-permute-start(bf16[16,32,640]{2,1,0:T(8,128)(2,1)} %fusion.44), channel_id=1, source_target_pairs={{64,0},{65,1},{66,2},{67,3},{68,4},{69,5},{70,6},{71,7},{72,8},{73... | collective-permute-start | bytes 1966088 | tf_op jit(solution)/shard_map/ppermute | solution.py:29
  117.0 5.1 %collective-permute-start.3 = (bf16[1,32,640]{2,1,0:T(8,128)(2,1)S(1)}, bf16[1,32,640]{2,1,0:T(8,128)(2,1)S(1)}, u32[]{:S(2)}, u32[]{:S(2)}) collective-permute-start(bf16[1,32,640]{2,1,0:T(8,128)(2,1)S(1)} %get-tuple-element.75), channel_id=1, source_target_pairs={{0,1},{2,3},{4,5},{6,7},{8,9},{10,11},{12,13},{14,15},{16,17},{18,... | collective-permute-start | bytes 122888 | tf_op jit(solution)/shard_map/ppermute | solution.py:20
  120.5 5.9 %collective-permute-start.4 = (bf16[1,32,640]{2,1,0:T(8,128)(2,1)S(1)}, bf16[1,32,640]{2,1,0:T(8,128)(2,1)S(1)}, u32[]{:S(2)}, u32[]{:S(2)}) collective-permute-start(bf16[1,32,640]{2,1,0:T(8,128)(2,1)S(1)} %get-tuple-element.76), channel_id=1, source_target_pairs={{1,0},{3,2},{5,4},{7,6},{9,8},{11,10},{13,12},{15,14},{17,16},{19,... | collective-permute-start | bytes 122888 | tf_op jit(solution)/shard_map/ppermute | solution.py:21
  122.0 6.2 %copy-start.10 = (f32[512,640]{1,0:T(8,128)}, f32[512,640]{1,0:T(8,128)S(1)}, u32[]{:S(2)}) copy-start(f32[512,640]{1,0:T(8,128)S(1)} %multiply_add_fusion.1) | copy-start | bytes 3932164
  128.2 13.3 %copy-start.11 = (bf16[512,9,640]{2,0,1:T(8,128)(2,1)}, bf16[512,9,640]{2,0,1:T(8,128)(2,1)S(1)}, u32[]{:S(2)}) copy-start(bf16[512,9,640]{2,0,1:T(8,128)(2,1)S(1)} %constant_dynamic-update-slice_fusion.9) | copy-start | bytes 17694724
  150.0 15.8 %collective-permute-start.5 = (bf16[16,32,640]{2,1,0:T(8,128)(2,1)}, bf16[16,32,640]{2,1,0:T(8,128)(2,1)S(1)}, u32[]{:S(2)}, u32[]{:S(2)}) collective-permute-start(bf16[16,32,640]{2,1,0:T(8,128)(2,1)} %fusion.34), channel_id=1, source_target_pairs={{64,0},{65,1},{66,2},{67,3},{68,4},{69,5},{70,6},{71,7},{72,8},{73... | collective-permute-start | bytes 1966088 | tf_op jit(solution)/shard_map/ppermute | solution.py:29
  151.6 14.2 %copy-start.3 = (bf16[2,16,32,640]{3,2,1,0:T(8,128)(2,1)S(1)}, bf16[2,16,32,640]{3,2,1,0:T(8,128)(2,1)}, u32[]{:S(2)}) copy-start(bf16[2,16,32,640]{3,2,1,0:T(8,128)(2,1)} %param.10) | copy-start | bytes 3932164
  166.1 3.8 collective-permute-start.6
  168.3 5.9 %collective-permute-start.7 = (bf16[1,32,640]{2,1,0:T(8,128)(2,1)S(1)}, bf16[1,32,640]{2,1,0:T(8,128)(2,1)S(1)}, u32[]{:S(2)}, u32[]{:S(2)}) collective-permute-start(bf16[1,32,640]{2,1,0:T(8,128)(2,1)S(1)} %get-tuple-element.72), channel_id=1, source_target_pairs={{1,0},{3,2},{5,4},{7,6},{9,8},{11,10},{13,12},{15,14},{17,16},{19,... | collective-permute-start | bytes 122888 | tf_op jit(solution)/shard_map/ppermute | solution.py:21
  169.7 13.5 %copy-start.5 = (f32[512,640]{1,0:T(8,128)}, f32[512,640]{1,0:T(8,128)S(1)}, u32[]{:S(2)}) copy-start(f32[512,640]{1,0:T(8,128)S(1)} %fusion.29) | copy-start | bytes 3932164
  204.0 292.3 %all-reduce.12.cloned.1.call-start = ((), (), s32[]{:S(2)}) async-start(), calls=%async_computation | async-start | bytes 1105920 | tf_op jit(solution)/shard_map/psum | solution.py:116
  206.0 2.5 copy-start.2
  206.0 2.5 copy-start.4
  206.0 2.9 copy-start.8
  (2 other events, 2.4 us)
Sparse Core Ops, SparseCore 0:
  10.8 66.3 all-gather.2
  204.2 141.2 all-reduce.13
  347.9 36.9 all-reduce.11
where the time goes:
time: 513 us; the launch traced here: 506 us
  waiting for transfers between devices  174 us (34%)
  blocking collectives  166 us (32%)
  matrix products  84.5 us (16%)
  local copies, waits for them, and re-layouts  30.6 us (6%)
  other arithmetic  18.2 us (4%)
  starting transfers between devices  16.7 us (3%)
  between operations  15.5 us (3%)
    psum x1, blocking collectives, shards(): gain_grad, shift_grad = lax.psum((gain_grad, shift_grad), ('dp', 'rows'))  145 us
    unnamed x4, waiting for transfers between devices  115 us
    dot_general x3, matrix products, shards(): jnp.einsum('pi,pko->iko', active, shifted, preferred_element_type=jnp.flo...  45.3 us
    all_gather x1, waiting for transfers between devices, shards(): lax.all_gather(weight_local, 'dp', axis=1, tiled=True)  43.2 us
    dot_general x3, matrix products, project(): jnp.einsum('pko,kio->pi', shifted, piece_rows, preferred_element_type=jnp...  39.1 us
    unnamed x58, local copies, waits for them, and re-layouts  22.4 us
    psum x3, blocking collectives, shards(): lax.psum((jnp.sum(norm_grad, axis=(0, 2)), jnp.sum(norm_grad * norm_group...  15 us
  transfers between devices with their start and end apart: 11, of which 8 were waited for; matrix products, arithmetic and copies ran while one was open for 12% of the time, Pallas kernels for 0%

commit v1 on v0

v1 whole, which is shorter than its diff:
```python
import jax
import jax.numpy as jnp
import numpy as np
from jax import lax
from jax.experimental import pallas as pl
from jax.experimental.pallas import tpu as pltpu
from jax.sharding import PartitionSpec as P

GROUPS = 16
epsilon = 1e-05
F32 = jnp.float32
BF16 = jnp.bfloat16

CH = 640
PX = 1024
HALF = 512
COLS = 32
LOCAL = 160
SHARD = 10
TAPS = [(-1, -1), (-1, 0), (-1, 1), (0, -1), (0, 0), (0, 1), (1, -1), (1, 0), (1, 1)]

AX, BX, AY, BY = 1, 3, 4, 12
ORDERS = [(AX, BX, AY, BY), (BX, AX, BY, AY), (AY, BY, AX, BX), (BY, AY, BX, AX)]
GATHER_PARTS = [((0, 1, 2, 3, 4), 0), ((5, 6, 7, 8), 2)]
SCATTER_PARTS = [((0, 3), 0), ((1, 4), 1), ((2, 5), 2), ((6, 7, 8), 3)]

VMEM = 58 * 1024 * 1024


def slot_masks(order):
    return [
        (u >> 3 & 1) * order[0] ^ (u >> 2 & 1) * order[1] ^ (u >> 1 & 1) * order[2] ^ (u & 1) * order[3]
        for u in range(16)
    ]


def reorder(order):
    here, base = slot_masks(ORDERS[order]), slot_masks(ORDERS[0])
    out = np.zeros((LOCAL, LOCAL), np.float32)
    for u in range(16):
        v = base.index(here[u])
        for i in range(SHARD):
            out[u * SHARD + i, v * SHARD + i] = 1.0
    return out


def flip(a, mask):
    return lax.ppermute(a, "dp", [(i, i ^ mask) for i in range(32)])


def chip(a, mask):
    return flip(a, mask << 1)


def core(a):
    return flip(a, 1)


def rows(a):
    return lax.ppermute(a, "rows", [(0, 1), (1, 0)])


def along_z(a, pairs):
    return lax.ppermute(a, ("segment", "rows"), pairs)


def lanes(shape):
    return lax.broadcasted_iota(jnp.int32, shape, 1)


def rows_on(tiles, dr, low):
    if not dr:
        return tiles
    lane = lanes(tiles[0].shape)
    edge, step = (3, COLS) if dr > 0 else (0, 128 - COLS)
    here, there = (pltpu.roll(tiles[h * 4 + edge], step, 1) for h in (0, 1))
    inner = lane >= COLS if dr > 0 else lane < 128 - COLS
    upper = 1.0 - low
    to_here, to_there = (low, upper) if dr > 0 else (upper, low)
    ends = (jnp.where(inner, here, there * to_here), jnp.where(inner, there, here * to_there))
    out = []
    for h in (0, 1):
        part = tiles[h * 4 : h * 4 + 4]
        out += [ends[h], *part[:3]] if dr > 0 else [*part[1:], ends[h]]
    return out


def columns_on(tiles, dc):
    if not dc:
        return tiles
    col = lanes(tiles[0].shape) & (COLS - 1)
    valid = col >= 1 if dc > 0 else col <= COLS - 2
    return [jnp.where(valid, pltpu.roll(t, dc % 128, 1), 0.0) for t in tiles]


def added(one, other):
    return other if one is None else [a + b for a, b in zip(one, other)]


def tiles_of(ref, at, size):
    return [ref[pl.ds(at, size), t * 128 : (t + 1) * 128] for t in range(8)]


def columns_of(coef):
    return [jnp.broadcast_to(coef[:, i : i + 1], (coef.shape[0], 128)) for i in range(4)]


def assemble_body(fix_ref, *refs):
    parts, out_ref = refs[:-1], refs[-1]
    for p, (taps, order) in enumerate(GATHER_PARTS):
        own, far = parts[2 * p : 2 * p + 2]
        for t, k in enumerate(taps):
            at = slice(t * CH, (t + 1) * CH)
            if order:
                both = jnp.concatenate([own[:, at], far[:, at]], axis=0)
                out_ref[k * LOCAL : (k + 1) * LOCAL, :] = jnp.dot(
                    fix_ref[...], both, preferred_element_type=F32
                ).astype(BF16)
            else:
                out_ref[k * LOCAL : k * LOCAL + LOCAL // 2, :] = own[:, at]
                out_ref[k * LOCAL + LOCAL // 2 : (k + 1) * LOCAL, :] = far[:, at]


def call(body, args, outs, scratch, name, flops, in_bytes, aliases=None, scalars=()):
    return pl.pallas_call(
        body,
        in_specs=[pl.BlockSpec(memory_space=pltpu.SMEM)] * len(scalars)
        + [pl.BlockSpec(memory_space=pltpu.VMEM)] * len(args),
        out_specs=[pl.BlockSpec(memory_space=pltpu.VMEM)] * len(outs),
        out_shape=[jax.ShapeDtypeStruct(shape, dtype) for shape, dtype in outs],
        scratch_shapes=scratch,
        input_output_aliases=aliases or {},
        compiler_params=pltpu.CompilerParams(vmem_limit_bytes=VMEM),
        cost_estimate=pl.CostEstimate(flops=flops, bytes_accessed=in_bytes, transcendentals=0),
        name=name,
    )(*scalars, *args)


def back_body(low_ref, g0_ref, g1_ref, w_ref, a_ref, coef_ref, pre_ref, sums_ref, y_ref):
    low = low_ref[0].astype(F32)
    for k in range(9):
        for h, g_ref in enumerate((g0_ref, g1_ref)):
            y_ref[k * LOCAL : (k + 1) * LOCAL, h * HALF : (h + 1) * HALF] = jnp.dot(
                w_ref[k * LOCAL : (k + 1) * LOCAL, :], g_ref[...], preferred_element_type=F32
            )

    def strip(i, carry):
        at = pl.multiple_of(i * 8, 8)
        total = None
        for dc in (-1, 0, 1):
            part = None
            for dr in (-1, 0, 1):
                k = (dr + 1) * 3 + dc + 1
                part = added(part, rows_on(tiles_of(y_ref, k * LOCAL + at, 8), dr, low))
            total = added(total, columns_on(part, dc))
        mean, inv, gain, shift = columns_of(coef_ref[pl.ds(at, 8), :])
        s0, s1 = jnp.zeros((8, 128), F32), jnp.zeros((8, 128), F32)
        for t in range(8):
            a = a_ref[pl.ds(at, 8), t * 128 : (t + 1) * 128].astype(F32)
            normed = (a - mean) * inv
            preact = normed * gain + shift
            gate = jax.nn.sigmoid(preact)
            pre = total[t] * (gate * (1.0 + preact * (1.0 - gate)))
            pre_ref[pl.ds(at, 8), t * 128 : (t + 1) * 128] = pre
            s0, s1 = s0 + pre, s1 + pre * normed
        s0, s1 = jnp.sum(s0, axis=1, keepdims=True), jnp.sum(s1, axis=1, keepdims=True)
        lane = lanes((8, 128))
        sums_ref[pl.ds(at, 8), :] = jnp.where(lane == 0, s0, jnp.where(lane == 1, s1, 0.0))
        return carry

    lax.fori_loop(0, LOCAL // 8, strip, 0, unroll=4)


def back(low, g0, g1, w, a, coef):
    return call(
        back_body,
        (g0, g1, w, a, coef),
        [((LOCAL, PX), F32), ((LOCAL, 128), F32)],
        [pltpu.VMEM((9 * LOCAL, PX), F32)],
        "back",
        2 * 9 * LOCAL * CH * PX,
        5_000_000,
        scalars=(low,),
    )


def wgrad_body(accumulate, flags_ref, order_ref, unpick_ref, *refs):
    refs = list(refs)
    samples = [[refs.pop(0) for _ in range(8)] for _ in range(2)]
    count = 2 * len(SCATTER_PARTS)
    before = [refs.pop(0) for _ in range(count)] if accumulate else None
    outs = [refs.pop(0) for _ in range(count)]
    full = [[refs.pop(0) for _ in range(2)] for _ in range(2)]
    plain, ordered, shifted, adjoint = refs
    low = flags_ref[0].astype(F32)
    section = flags_ref[1]
    for o, (g0, g1, s00, s01, s10, s11, a_ref, coef_ref) in enumerate(samples):

        @pl.when(section == 1)
        def _():
            for h, g in enumerate((g0, g1)):
                full[o][h][...] = g[...]

        @pl.when(section == 0)
        def _():
            for h in (0, 1):
                total = None
                for b, (s, turned) in enumerate(((s00, 0), (s01, 1), (s10, 0), (s11, 1))):
                    at = (h ^ turned) * HALF
                    part = jnp.dot(
                        unpick_ref[b], s[:, at : at + HALF], preferred_element_type=F32
                    )
                    total = part if total is None else total + part
                full[o][h][...] = total.astype(BF16)

        for h in (0, 1):
            adjoint[:, o * PX + h * HALF : o * PX + (h + 1) * HALF] = full[o][h][...]

        def activate(i, carry):
            at = pl.multiple_of(i * 16, 16)
            mean, inv, gain, shift = columns_of(coef_ref[pl.ds(at, 16), :])
            for t in range(8):
                a = a_ref[pl.ds(at, 16), t * 128 : (t + 1) * 128].astype(F32)
                preact = (a - mean) * inv * gain + shift
                plain[pl.ds(at, 16), t * 128 : (t + 1) * 128] = (
                    preact * jax.nn.sigmoid(preact)
                ).astype(BF16)
            return carry

        lax.fori_loop(0, LOCAL // 16, activate, 0, unroll=5)
        for p, (taps, _) in enumerate(SCATTER_PARTS):
            ordered[...] = jnp.dot(order_ref[p], plain[...], preferred_element_type=F32)

            def build(i, carry):
                at = pl.multiple_of(i * 16, 16)
                tiles = tiles_of(ordered, at, 16)
                moved = {}
                for k in taps:
                    dr, dc = TAPS[k]
                    if dc not in moved:
                        moved[dc] = columns_on(tiles, -dc)
                    for t, y in enumerate(rows_on(moved[dc], -dr, low)):
                        at_px = o * PX + t * 128
                        shifted[pl.ds(k * LOCAL + at, 16), at_px : at_px + 128] = y.astype(BF16)
                return carry

            lax.fori_loop(0, LOCAL // 16, build, 0, unroll=5)
    for p, (taps, _) in enumerate(SCATTER_PARTS):
        for t, k in enumerate(taps):
            value = lax.dot_general(
                shifted[k * LOCAL : (k + 1) * LOCAL, :],
                adjoint[...],
                (((1,), (1,)), ((), ())),
                preferred_element_type=F32,
            )
            for side in (0, 1):
                part = value[side * LOCAL // 2 : (side + 1) * LOCAL // 2]
                at = slice(t * CH, (t + 1) * CH)
                if accumulate:
                    part = part + before[2 * p + side][:, at]
                outs[2 * p + side][:, at] = part


def wgrad(flags, unpick, samples, before=()):
    orders = jnp.asarray(np.stack([reorder(o) for _, o in SCATTER_PARTS]), BF16)
    outs = [((LOCAL // 2, len(taps) * CH), F32) for taps, _ in SCATTER_PARTS for _ in (0, 1)]
    args = [orders, unpick, *samples[0], *samples[1], *before]
    aliases = {1 + len(args) - len(before) + i: i for i in range(len(before))}
    got = call(
        lambda *refs: wgrad_body(bool(before), *refs),
        args,
        outs + [((CH, HALF), BF16)] * 4,
        [
            pltpu.VMEM((LOCAL, PX), BF16),
            pltpu.VMEM((LOCAL, PX), F32),
            pltpu.VMEM((9 * LOCAL, 2 * PX), BF16),
            pltpu.VMEM((CH, 2 * PX), BF16),
        ],
        "wgrad",
        2 * 2 * 9 * LOCAL * CH * PX,
        10_000_000,
        aliases,
        scalars=(flags,),
    )
    return got[: len(outs)], (got[-4:-2], got[-2:])


def spread(groups):
    return jnp.broadcast_to(groups[..., None], (*groups.shape, SHARD)).reshape(*groups.shape[:-1], LOCAL)


def slots(channels):
    return jnp.sum(channels.reshape(*channels.shape[:-1], 16, SHARD), axis=-1)


def over_four(x):
    x = x + core(x)
    return x + rows(x)


def turn_rows(a):
    return jnp.swapaxes(a.reshape(2, 4, 4, COLS, CH), 1, 2).reshape(2, HALF, CH)


def shards(segment_inputs, weights, gains, shifts, chain_cot, skip_cot):
    count_all = float(PX * CH // GROUPS)
    seg = lax.axis_index("segment")
    dp = lax.axis_index("dp")
    r = lax.axis_index("rows")
    c = dp % 2
    me = dp // 2
    low = jnp.stack([r, seg]).astype(jnp.int32)

    mine = lax.dynamic_slice_in_dim(weights[0], r * SHARD, SHARD, axis=1)
    gathered = [
        jnp.transpose(mine[taps[0] : taps[-1] + 1], (1, 0, 2)).reshape(SHARD, -1)
        for taps, _ in GATHER_PARTS
    ]
    for stage in (3, 2, 1):
        gathered = [
            jnp.concatenate([cur, chip(cur, ORDERS[order][stage])], axis=0)
            for cur, (_, order) in zip(gathered, GATHER_PARTS)
        ]
    weight_parts = []
    for cur, (_, order) in zip(gathered, GATHER_PARTS):
        weight_parts += [cur, chip(cur, ORDERS[order][0])]
    fix = jnp.asarray(reorder(GATHER_PARTS[1][1]).T, BF16)

    row = np.arange(CH)
    flips = np.asarray(slot_masks(ORDERS[0]))[row // SHARD % 16]
    natural = (
        40 * (me ^ jnp.asarray(flips, jnp.int32))
        + 20 * (c ^ jnp.asarray(row // 320, jnp.int32))
        + 10 * (r ^ jnp.asarray(row // LOCAL % 2, jnp.int32))
        + jnp.asarray(row % SHARD, jnp.int32)
    )
    hit = natural[:, None] == lax.broadcasted_iota(jnp.int32, (CH, CH), 1)
    pick = hit.astype(BF16)
    own_hit = hit[:LOCAL]
    eye = jnp.eye(CH, dtype=BF16)
    column = natural.reshape(4, 1, LOCAL)
    unpick = (column == lax.broadcasted_iota(jnp.int32, (4, CH, LOCAL), 1)).astype(BF16)

    total = chain_cot.astype(F32) + skip_cot.astype(F32)
    flat = turn_rows(total.astype(BF16))
    outer_t = jnp.einsum("ij,npj->nip", eye, flat, preferred_element_type=F32).astype(BF16)
    outer = []
    for n in range(2):
        near = outer_t[n]
        far = along_z(near, [(2, 3), (3, 2)] if n == 0 else [(1, 2), (0, 3)])
        outer.append(((near, far), (core(near), core(far))))

    local = turn_rows(segment_inputs[0])
    picked = jnp.einsum("ij,npj->nip", pick, local, preferred_element_type=F32).astype(BF16)
    picked = picked.reshape(2, 2, 2, LOCAL, HALF)
    both = jnp.concatenate([picked[:, :, 0], rows(picked[:, :, 1])], axis=-1)
    theirs = core(both[:, 1])
    inputs = [(both[n, 0], theirs[n]) for n in range(2)]

    sums = []
    for n in range(2):
        for o in range(2):
            wide = inputs[n][o].astype(F32)
            sums.append(jnp.stack([jnp.sum(wide, -1), jnp.sum(wide * wide, -1)]))
    local_sums = slots(jnp.stack(sums).reshape(2, 2, 2, LOCAL))
    local_sums = local_sums + core(local_sums)[:, ::-1]
    local_sums = local_sums + rows(local_sums)
    mean = local_sums[:, :, 0] / count_all
    inv = lax.rsqrt(local_sums[:, :, 1] / count_all - mean * mean + epsilon)
    gain = jnp.sum(jnp.where(own_hit, gains[0][None, :], 0.0), axis=1)
    shift = jnp.sum(jnp.where(own_hit, shifts[0][None, :], 0.0), axis=1)
    mean_c, inv_c = spread(mean), spread(inv)
    coef = jnp.stack(
        [mean_c, inv_c, jnp.broadcast_to(gain, mean_c.shape), jnp.broadcast_to(shift, mean_c.shape)],
        axis=-1,
    )
    coef = jnp.pad(coef, ((0, 0), (0, 0), (0, 0), (0, 124)))

    (w,) = call(
        assemble_body, (fix, *weight_parts), [((9 * LOCAL, CH), BF16)], [], "assemble", 10**8, 4_000_000
    )

    def in_grads(n, halves):
        pres, parts = [], []
        for o in range(2):
            pre, part = back(low, *halves[o], w, inputs[n][o], coef[n, o])
            pres.append(pre)
            parts.append(part[:, :2])
        s = jnp.stack(parts)
        group = slots(jnp.moveaxis(s * gain[None, :, None], 2, 1))
        group = group + core(group)[::-1]
        group = group + rows(group)
        grads = []
        for o in range(2):
            first = spread(group[o, 0] / count_all)[:, None]
            second = spread(group[o, 1] / count_all)[:, None]
            normed = (inputs[n][o].astype(F32) - mean_c[n, o][:, None]) * inv_c[n, o][:, None]
            grads.append(
                inv_c[n, o][:, None] * (pres[o] * gain[:, None] - first - normed * second)
            )
        return grads, s

    slices = []
    for n in range(2):
        grads, _ = in_grads(n, outer[n])
        got = []
        for o in range(2):
            one = along_z(grads[o].astype(BF16), [(2, 1), (3, 0)])
            got.append((along_z(one, [(0, 1), (1, 0)]), one))
        across = [tuple(core(a) for a in got[o]) for o in range(2)]
        slices.append([(*got[o], *across[1 - o]) for o in range(2)])

    weight_grads, adjoint = (), []
    for n in range(2):
        samples = [
            (*outer[n][o], *slices[n][o], inputs[n][o], coef[n, o]) for o in range(2)
        ]
        weight_grads, full = wgrad(low, unpick, samples, weight_grads)
        adjoint.append(full)

    scattered = []
    for p, (_, order) in enumerate(SCATTER_PARTS):
        keep, give = weight_grads[2 * p : 2 * p + 2]
        for stage in range(4):
            cur = keep + chip(give, ORDERS[order][stage])
            half = cur.shape[0] // 2
            keep, give = cur[:half], cur[half:]
        scattered.append(cur)
    taps = [k for part, _ in SCATTER_PARTS for k in part]
    shard = jnp.concatenate(scattered, axis=1).reshape(SHARD, 9, CH)
    shard = jnp.stack([shard[:, taps.index(k)] for k in range(9)])
    far_shard = rows(shard)
    weight_grad = jnp.where(
        r == 0,
        jnp.concatenate([shard, far_shard], axis=1),
        jnp.concatenate([far_shard, shard], axis=1),
    )

    results, norm_sums = [], 0.0
    for n in range(2):
        grads, s = in_grads(n, adjoint[n])
        norm_sums = norm_sums + jnp.sum(s, axis=0)
        split = []
        for o in range(2):
            high = lax.reduce_precision(grads[o], 8, 7)
            split.append(jnp.stack([high, grads[o] - high]).astype(BF16))
        two = jnp.stack([split[0], core(split[1])], axis=1)
        two = jnp.stack([two[..., :HALF], rows(two[..., HALF:])], axis=2).reshape(2, CH, HALF)
        nat = jnp.einsum("tjp,ji->tpi", two, pick, preferred_element_type=F32)
        nat = jnp.swapaxes(nat.reshape(2, 4, 4, COLS, CH), 1, 2).reshape(2, HALF // COLS, COLS, CH)
        wide = chain_cot[n].astype(F32) + skip_cot[n].astype(F32)
        results.append((nat[0] + jnp.where(seg == 0, nat[1] + wide, 0.0)).astype(BF16))
    outputs = jnp.stack(results)[None]

    spread_sums = jnp.sum(jnp.where(own_hit[:, None, :], norm_sums[:, :, None], 0.0), axis=0)
    for mask in (1, 2, 6, 8, 24):
        spread_sums = spread_sums + flip(spread_sums, mask)
    spread_sums = spread_sums + rows(spread_sums)
    return (outputs, weight_grad[None], spread_sums[1][None], spread_sums[0][None])


def solution(mesh):
    placed = (
        P("segment", "dp", "rows", None, None),
        P("segment", None, "dp", None),
        P("segment", None),
        P("segment", None),
        P("dp", "rows", None, None),
        P("dp", "rows", None, None),
    )
    return jax.shard_map(
        shards,
        mesh=mesh,
        in_specs=placed,
        out_specs=(
            P("segment", "dp", "rows", None, None),
            P("segment", None, "dp", None),
            P("segment", None),
            P("segment", None),
        ),
        check_vma=False,
    )
```

time: 513 us -> 359 us (0.70)
  blocking collectives: 166 us -> 0 us
  Pallas kernels: 0 us -> 107 us
  matrix products: 84.5 us -> 6.61 us
  waiting for transfers between devices: 174 us -> 102 us
  starting transfers between devices: 16.7 us -> 83.8 us
  between operations: 15.5 us -> 2.43 us
  other arithmetic: 18.2 us -> 25.6 us
    psum x5 -> x0, blocking collectives: 166 us -> none  [the longest x1 145 us: shards(): gain_grad, shift_grad = lax.psum((gain_grad, shift_grad), ('dp', 'rows'))]
    unnamed x4 -> x0, waiting for transfers between devices: 115 us -> none
    pallas_call x0 -> x11, Pallas kernels: none -> 107 us  [call(): pl.pallas_call(body, in_specs=[pl.BlockSpec(memory_space=pltpu.SMEM)] * l...]
    ppermute x8 -> x69, waiting for transfers between devices: 16 us -> 102 us  [the longest x49 62.2 us: flip(): return lax.ppermute(a, 'dp', [(i, i ^ mask) for i in range(32)])]
    dot_general x6 -> x4, matrix products: 84.5 us -> 6.61 us  [the longest x2 4.16 us: shards(): nat = jnp.einsum('tjp,ji->tpi', two, pick, preferred_element_type=F32)]
    ppermute x8 -> x69, starting transfers between devices: 16.3 us -> 83.8 us  [the longest x10 39.6 us: along_z(): return lax.ppermute(a, ('segment', 'rows'), pairs)]
    all_gather x1 -> x0, waiting for transfers between devices: 43.2 us -> none  [shards(): lax.all_gather(weight_local, 'dp', axis=1, tiled=True)]
    unnamed x58 -> x101, local copies, waits for them, and re-layouts: 22.4 us -> 6.86 us
  transfers between devices with their start and end apart: 11 -> 69, of which waited for: 8 -> 30; matrix products, arithmetic and copies ran while one was open for 12% -> 13% of each run, Pallas kernels for 0% -> 17%
where the time goes in v1:
time: 359 us; the launch traced here: 356 us
  Pallas kernels  107 us (30%)
  waiting for transfers between devices  102 us (28%)
  starting transfers between devices  83.8 us (23%)
  local copies, waits for them, and re-layouts  28.4 us (8%)
  other arithmetic  25.6 us (7%)
  matrix products  6.61 us (2%)
    pallas_call x11, Pallas kernels, call(): pl.pallas_call(body, in_specs=[pl.BlockSpec(memory_space=pltpu.SMEM)] * l...  107 us
    ppermute x49, waiting for transfers between devices, flip(): return lax.ppermute(a, 'dp', [(i, i ^ mask) for i in range(32)])  62.2 us
    ppermute x10, starting transfers between devices, along_z(): return lax.ppermute(a, ('segment', 'rows'), pairs)  39.6 us
    ppermute x49, starting transfers between devices, flip(): return lax.ppermute(a, 'dp', [(i, i ^ mask) for i in range(32)])  35.6 us
    ppermute x10, waiting for transfers between devices, along_z(): return lax.ppermute(a, ('segment', 'rows'), pairs)  24.3 us
    ppermute x10, waiting for transfers between devices, rows(): return lax.ppermute(a, 'rows', [(0, 1), (1, 0)])  15.9 us
    ppermute x10, starting transfers between devices, rows(): return lax.ppermute(a, 'rows', [(0, 1), (1, 0)])  8.57 us
  transfers between devices with their start and end apart: 69, of which 30 were waited for; matrix products, arithmetic and copies ran while one was open for 13% of the time, Pallas kernels for 17%

profile of v1, /device:TPU:0, one launch (start us, length us, event | category | flops | bytes accessed | tf_op | source)
XLA Modules:
  0.0 355.9 jit_solution(9728443402277438781)
XLA Ops:
  5.3 6.9 %collective-permute-start.29 = (bf16[640,512]{1,0:T(8,128)(2,1)}, bf16[640,512]{1,0:T(8,128)(2,1)}, u32[]{:S(2)}, u32[]{:S(2)}) collective-permute-start(bf16[640,512]{1,0:T(8,128)(2,1)} %get-tuple-element.127.g0_ref.refs_3_), channel_id=1, source_target_pairs={{1,64},{0,65},{3,66},{2,67},{5,68},{4,69},{7,70},{6,71},{9,72},{8,... | collective-permute-start | bytes 1966088 | tf_op jit(solution)/shard_map/ppermute | solution.py:64
  25.5 4.5 %collective-permute-done.10 = bf16[20,2560]{1,0:T(8,128)(2,1)S(1)} collective-permute-done((bf16[20,2560]{1,0:T(8,128)(2,1)S(1)}, bf16[20,2560]{1,0:T(8,128)(2,1)S(1)}, u32[]{:S(2)}, u32[]{:S(2)}) %collective-permute-start.10) | collective-permute-done | bytes 102432 | tf_op jit(solution)/shard_map/ppermute | solution.py:48
  30.3 5.0 %collective-permute-done.6 = bf16[20,3200]{1,0:T(8,128)(2,1)S(1)} collective-permute-done((bf16[20,3200]{1,0:T(8,128)(2,1)S(1)}, bf16[20,3200]{1,0:T(8,128)(2,1)S(1)}, u32[]{:S(2)}, u32[]{:S(2)}) %collective-permute-start.6) | collective-permute-done | bytes 128032 | tf_op jit(solution)/shard_map/ppermute | solution.py:48
  46.0 9.8 %collective-permute-done.12.refs_3_ = bf16[80,2560]{1,0:T(8,128)(2,1)S(1)} collective-permute-done((bf16[80,2560]{1,0:T(8,128)(2,1)S(1)}, bf16[80,2560]{1,0:T(8,128)(2,1)S(1)}, u32[]{:S(2)}, u32[]{:S(2)}) %collective-permute-start.12) | collective-permute-done | bytes 409632 | tf_op jit(solution)/shard_map/ppermute | solution.py:48
  65.6 7.3 %back.12 = (f32[160,1024]{1,0:T(8,128)}, f32[160,128]{1,0:T(8,128)}) custom-call(s32[2]{0:T(128)} %pad_add_fusion.low_ref.refs_0_, bf16[640,512]{1,0:T(8,128)(2,1)} %get-tuple-element.127.g0_ref.refs_3_, bf16[640,512]{1,0:T(8,128)(2,1)} %collective-permute-done.29.g1_ref.refs_4_, bf16[1440,640]{1,0:T(8,128)(2,1)} %assemble.1.w_ref, ...), custom_call_target="tpu_custom_call" | custom-call | flops 1887436800 | bytes 5000000 | tf_op jit(solution)/shard_map/back/pallas_call | solution.py:125
  74.7 7.3 %back.13 = (f32[160,1024]{1,0:T(8,128)}, f32[160,128]{1,0:T(8,128)}) custom-call(s32[2]{0:T(128)} %pad_add_fusion.low_ref.refs_0_, bf16[640,512]{1,0:T(8,128)(2,1)} %collective-permute-done.30.g0_ref.refs_11_, bf16[640,512]{1,0:T(8,128)(2,1)} %copy-done.36, bf16[1440,640]{1,0:T(8,128)(2,1)} %assemble.1.w_ref, ...), custom_call_target="tpu_custom_call" | custom-call | flops 1887436800 | bytes 5000000 | tf_op jit(solution)/shard_map/back/pallas_call | solution.py:125
  83.2 7.3 %back.8 = (f32[160,1024]{1,0:T(8,128)}, f32[160,128]{1,0:T(8,128)}) custom-call(s32[2]{0:T(128)} %pad_add_fusion.low_ref.refs_0_, bf16[640,512]{1,0:T(8,128)(2,1)} %get-tuple-element.126.g0_ref.refs_3_, bf16[640,512]{1,0:T(8,128)(2,1)} %collective-permute-done.4.g1_ref.refs_4_, bf16[1440,640]{1,0:T(8,128)(2,1)} %assemble.1.w_ref, ...), custom_call_target="tpu_custom_call" | custom-call | flops 1887436800 | bytes 5000000 | tf_op jit(solution)/shard_map/back/pallas_call | solution.py:125
  91.5 7.3 %back.9 = (f32[160,1024]{1,0:T(8,128)}, f32[160,128]{1,0:T(8,128)}) custom-call(s32[2]{0:T(128)} %pad_add_fusion.low_ref.refs_0_, bf16[640,512]{1,0:T(8,128)(2,1)} %collective-permute-done.13.g0_ref.refs_11_, bf16[640,512]{1,0:T(8,128)(2,1)} %collective-permute-done.14.g1_ref.refs_12_, bf16[1440,640]{1,0:T(8,128)(2,1)} %assemble.1.w_ref, ...), custom_call_target="tpu_custom_call" | custom-call | flops 1887436800 | bytes 5000000 | tf_op jit(solution)/shard_map/back/pallas_call | solution.py:125
  111.4 15.2 %collective-permute-start.19 = (bf16[160,1024]{1,0:T(8,128)(2,1)S(1)}, bf16[160,1024]{1,0:T(8,128)(2,1)S(1)}, u32[]{:S(2)}, u32[]{:S(2)}) collective-permute-start(bf16[160,1024]{1,0:T(8,128)(2,1)S(1)} %get-tuple-element.135), channel_id=1, source_target_pairs={{64,1},{65,0},{66,3},{67,2},{68,5},{69,4},{70,7},{71,6},{72,9},{73... | collective-permute-start | bytes 983048 | tf_op jit(solution)/shard_map/ppermute | solution.py:64
  133.1 6.7 %collective-permute-done.19.refs_14_ = bf16[160,1024]{1,0:T(8,128)(2,1)S(1)} collective-permute-done((bf16[160,1024]{1,0:T(8,128)(2,1)S(1)}, bf16[160,1024]{1,0:T(8,128)(2,1)S(1)}, u32[]{:S(2)}, u32[]{:S(2)}) %collective-permute-start.19) | collective-permute-done | bytes 327712 | tf_op jit(solution)/shard_map/ppermute | solution.py:64
  142.4 4.5 %collective-permute-done.36.refs_14_ = bf16[160,1024]{1,0:T(8,128)(2,1)S(1)} collective-permute-done((bf16[160,1024]{1,0:T(8,128)(2,1)S(1)}, bf16[160,1024]{1,0:T(8,128)(2,1)S(1)}, u32[]{:S(2)}, u32[]{:S(2)}) %collective-permute-start.36) | collective-permute-done | bytes 327712 | tf_op jit(solution)/shard_map/ppermute | solution.py:64
  146.8 5.1 %collective-permute-done.34.refs_6_ = bf16[160,1024]{1,0:T(8,128)(2,1)S(1)} collective-permute-done((bf16[160,1024]{1,0:T(8,128)(2,1)S(1)}, bf16[160,1024]{1,0:T(8,128)(2,1)S(1)}, u32[]{:S(2)}, u32[]{:S(2)}) %collective-permute-start.34) | collective-permute-done | bytes 327712 | tf_op jit(solution)/shard_map/ppermute | solution.py:64
  164.5 4.2 %collective-permute-done.35.refs_5_ = bf16[160,1024]{1,0:T(8,128)(2,1)S(1)} collective-permute-done((bf16[160,1024]{1,0:T(8,128)(2,1)S(1)}, bf16[160,1024]{1,0:T(8,128)(2,1)S(1)}, u32[]{:S(2)}, u32[]{:S(2)}) %collective-permute-start.35) | collective-permute-done | bytes 327712 | tf_op jit(solution)/shard_map/ppermute | solution.py:64
  169.2 21.6 %wgrad.2 = (f32[80,1280]{1,0:T(8,128)}, f32[80,1280]{1,0:T(8,128)}, f32[80,1280]{1,0:T(8,128)}, f32[80,1280]{1,0:T(8,128)}, f32[80,1280]{1,0:T(8,128)}, /*index=...) custom-call(s32[2]{0:T(128)} %pad_add_fusion.low_ref.refs_0_, ...), custom_call_target="tpu_custom_call" | custom-call | flops 3774873600 | bytes 10000000 | tf_op jit(solution)/shard_map/wgrad/pallas_call | solution.py:125
  190.9 7.3 %back.10 = (f32[160,1024]{1,0:T(8,128)}, f32[160,128]{1,0:T(8,128)}) custom-call(s32[2]{0:T(128)} %pad_add_fusion.low_ref.refs_0_, bf16[640,512]{1,0:T(8,128)(2,1)} %get-tuple-element.48.g0_ref, bf16[640,512]{1,0:T(8,128)(2,1)} %get-tuple-element.49.g1_ref, bf16[1440,640]{1,0:T(8,128)(2,1)} %assemble.1.w_ref, ...), custom_call_target="tpu_custom_call" | custom-call | flops 1887436800 | bytes 5000000 | tf_op jit(solution)/shard_map/back/pallas_call | solution.py:125
  198.2 7.3 %back.11 = (f32[160,1024]{1,0:T(8,128)}, f32[160,128]{1,0:T(8,128)}) custom-call(s32[2]{0:T(128)} %pad_add_fusion.low_ref.refs_0_, bf16[640,512]{1,0:T(8,128)(2,1)} %get-tuple-element.52.g0_ref, bf16[640,512]{1,0:T(8,128)(2,1)} %get-tuple-element.53.g1_ref, bf16[1440,640]{1,0:T(8,128)(2,1)} %assemble.1.w_ref, ...), custom_call_target="tpu_custom_call" | custom-call | flops 1887436800 | bytes 5000000 | tf_op jit(solution)/shard_map/back/pallas_call | solution.py:125
  206.6 23.4 %wgrad.3 = (f32[80,1280]{1,0:T(8,128)}, f32[80,1280]{1,0:T(8,128)}, f32[80,1280]{1,0:T(8,128)}, f32[80,1280]{1,0:T(8,128)}, f32[80,1280]{1,0:T(8,128)}, /*index=...) custom-call(s32[2]{0:T(128)} %pad_add_fusion.low_ref.refs_0_, ...), custom_call_target="tpu_custom_call", output_to_operand_aliasing={{0}: (19, {}), {1}: (20, {}), {2}: (21, {}), {3}: (22, {}),... | custom-call | flops 3774873600 | bytes 10000000 | tf_op jit(solution)/shard_map/wgrad/pallas_call | solution.py:125
  229.9 7.3 %back.14 = (f32[160,1024]{1,0:T(8,128)}, f32[160,128]{1,0:T(8,128)}) custom-call(s32[2]{0:T(128)} %pad_add_fusion.low_ref.refs_0_, bf16[640,512]{1,0:T(8,128)(2,1)} %get-tuple-element.68.g0_ref, bf16[640,512]{1,0:T(8,128)(2,1)} %get-tuple-element.69.g1_ref, bf16[1440,640]{1,0:T(8,128)(2,1)} %assemble.1.w_ref, ...), custom_call_target="tpu_custom_call" | custom-call | flops 1887436800 | bytes 5000000 | tf_op jit(solution)/shard_map/back/pallas_call | solution.py:125
  237.3 7.3 %back.15 = (f32[160,1024]{1,0:T(8,128)}, f32[160,128]{1,0:T(8,128)}) custom-call(s32[2]{0:T(128)} %pad_add_fusion.low_ref.refs_0_, bf16[640,512]{1,0:T(8,128)(2,1)} %get-tuple-element.72.g0_ref, bf16[640,512]{1,0:T(8,128)(2,1)} %get-tuple-element.73.g1_ref, bf16[1440,640]{1,0:T(8,128)(2,1)} %assemble.1.w_ref, ...), custom_call_target="tpu_custom_call" | custom-call | flops 1887436800 | bytes 5000000 | tf_op jit(solution)/shard_map/back/pallas_call | solution.py:125
  270.4 4.3 %collective-permute-done.65 = f32[2,640]{1,0:T(2,128)S(1)} collective-permute-done((f32[2,640]{1,0:T(2,128)S(1)}, f32[2,640]{1,0:T(2,128)S(1)}, u32[]{:S(2)}, u32[]{:S(2)}) %collective-permute-start.65) | collective-permute-done | bytes 5152 | tf_op jit(solution)/shard_map/ppermute | solution.py:48
  291.5 5.1 %collective-permute-done.47 = f32[40,1280]{1,0:T(8,128)S(1)} collective-permute-done((f32[40,1280]{1,0:T(8,128)S(1)}, f32[40,1280]{1,0:T(8,128)S(1)}, u32[]{:S(2)}, u32[]{:S(2)}) %collective-permute-start.47) | collective-permute-done | bytes 204832 | tf_op jit(solution)/shard_map/ppermute | solution.py:48
  299.9 4.7 %collective-permute-done.55 = f32[40,1280]{1,0:T(8,128)S(1)} collective-permute-done((f32[40,1280]{1,0:T(8,128)S(1)}, f32[40,1280]{1,0:T(8,128)S(1)}, u32[]{:S(2)}, u32[]{:S(2)}) %collective-permute-start.55) | collective-permute-done | bytes 204832 | tf_op jit(solution)/shard_map/ppermute | solution.py:48
  321.7 4.2 %collective-permute-done.60 = f32[20,1920]{1,0:T(8,128)S(1)} collective-permute-done((f32[20,1920]{1,0:T(8,128)S(1)}, f32[20,1920]{1,0:T(8,128)S(1)}, u32[]{:S(2)}, u32[]{:S(2)}) %collective-permute-start.60) | collective-permute-done | bytes 153632 | tf_op jit(solution)/shard_map/ppermute | solution.py:48
  336.3 4.9 %collective-permute-done.28 = bf16[2,2,160,512]{3,2,0,1:T(8,128)(2,1)} collective-permute-done((bf16[2,2,160,512]{3,2,0,1:T(8,128)(2,1)}, bf16[2,2,160,512]{3,2,0,1:T(8,128)(2,1)}, u32[]{:S(2)}, u32[]{:S(2)}) %collective-permute-start.28) | collective-permute-done | bytes 655392 | tf_op jit(solution)/shard_map/ppermute | solution.py:60
  (417 shorter events, 164.7 us)
Async XLA Ops:
  5.3 40.2 %collective-permute-start.29 = (bf16[640,512]{1,0:T(8,128)(2,1)}, bf16[640,512]{1,0:T(8,128)(2,1)}, u32[]{:S(2)}, u32[]{:S(2)}) collective-permute-start(bf16[640,512]{1,0:T(8,128)(2,1)} %get-tuple-element.127.g0_ref.refs_3_), channel_id=1, source_target_pairs={{1,64},{0,65},{3,66},{2,67},{5,68},{4,69},{7,70},{6,71},{9,72},{8,... | collective-permute-start | bytes 1966088 | tf_op jit(solution)/shard_map/ppermute | solution.py:64
  12.1 61.7 %collective-permute-start.30 = (bf16[640,512]{1,0:T(8,128)(2,1)}, bf16[640,512]{1,0:T(8,128)(2,1)}, u32[]{:S(2)}, u32[]{:S(2)}) collective-permute-start(bf16[640,512]{1,0:T(8,128)(2,1)} %get-tuple-element.127.g0_ref.refs_3_), channel_id=1, source_target_pairs={{0,2},{2,0},{4,6},{6,4},{8,10},{10,8},{12,14},{14,12},{16,18},{18,... | collective-permute-start | bytes 1966088 | tf_op jit(solution)/shard_map/ppermute | solution.py:48
  14.2 21.4 %collective-permute-start = (bf16[2,2,160,512]{3,2,1,0:T(8,128)(2,1)S(1)}, bf16[2,2,160,512]{3,2,1,0:T(8,128)(2,1)S(1)}, u32[]{:S(2)}, u32[]{:S(2)}) collective-permute-start(bf16[2,2,160,512]{3,2,1,0:T(8,128)(2,1)S(1)} %get-tuple-element.132), channel_id=1, source_target_pairs={{0,1},{1,0},{2,3},{3,2},{4,5},{5,4},{6,7},{7,6},{8,9},{9,8},{10,11... | collective-permute-start | bytes 1966088 | tf_op jit(solution)/shard_map/ppermute | solution.py:60
  23.5 22.0 %collective-permute-start.4 = (bf16[640,512]{1,0:T(8,128)(2,1)}, bf16[640,512]{1,0:T(8,128)(2,1)}, u32[]{:S(2)}, u32[]{:S(2)}) collective-permute-start(bf16[640,512]{1,0:T(8,128)(2,1)} %get-tuple-element.126.g0_ref.refs_3_), channel_id=1, source_target_pairs={{64,65},{65,64},{66,67},{67,66},{68,69},{69,68},{70,71},{71,70},{7... | collective-permute-start | bytes 1966088 | tf_op jit(solution)/shard_map/ppermute | solution.py:64
  45.5 46.0 %collective-permute-start.13 = (bf16[640,512]{1,0:T(8,128)(2,1)}, bf16[640,512]{1,0:T(8,128)(2,1)}, u32[]{:S(2)}, u32[]{:S(2)}) collective-permute-start(bf16[640,512]{1,0:T(8,128)(2,1)} %get-tuple-element.126.g0_ref.refs_3_), channel_id=1, source_target_pairs={{0,2},{2,0},{4,6},{6,4},{8,10},{10,8},{12,14},{14,12},{16,18},{18,... | collective-permute-start | bytes 1966088 | tf_op jit(solution)/shard_map/ppermute | solution.py:48
  45.6 28.3 %collective-permute-start.31 = (bf16[640,512]{1,0:T(8,128)(2,1)}, bf16[640,512]{1,0:T(8,128)(2,1)S(1)}, u32[]{:S(2)}, u32[]{:S(2)}) collective-permute-start(bf16[640,512]{1,0:T(8,128)(2,1)} %collective-permute-done.29.g1_ref.refs_4_), channel_id=1, source_target_pairs={{0,2},{2,0},{4,6},{6,4},{8,10},{10,8},{12,14},{14,12},{16,18},{18,... | collective-permute-start | bytes 1966088 | tf_op jit(solution)/shard_map/ppermute | solution.py:48
  55.9 35.6 %collective-permute-start.14 = (bf16[640,512]{1,0:T(8,128)(2,1)}, bf16[640,512]{1,0:T(8,128)(2,1)}, u32[]{:S(2)}, u32[]{:S(2)}) collective-permute-start(bf16[640,512]{1,0:T(8,128)(2,1)} %collective-permute-done.4.g1_ref.refs_4_), channel_id=1, source_target_pairs={{0,2},{2,0},{4,6},{6,4},{8,10},{10,8},{12,14},{14,12},{16,18},{18,... | collective-permute-start | bytes 1966088 | tf_op jit(solution)/shard_map/ppermute | solution.py:48
  107.3 21.9 %collective-permute-start.17 = (bf16[160,1024]{1,0:T(8,128)(2,1)}, bf16[160,1024]{1,0:T(8,128)(2,1)}, u32[]{:S(2)}, u32[]{:S(2)}) collective-permute-start(bf16[160,1024]{1,0:T(8,128)(2,1)} %fusion.30), channel_id=1, source_target_pairs={{64,1},{65,0},{66,3},{67,2},{68,5},{69,4},{70,7},{71,6},{72,9},{73... | collective-permute-start | bytes 983048 | tf_op jit(solution)/shard_map/ppermute | solution.py:64
  111.4 28.4 %collective-permute-start.19 = (bf16[160,1024]{1,0:T(8,128)(2,1)S(1)}, bf16[160,1024]{1,0:T(8,128)(2,1)S(1)}, u32[]{:S(2)}, u32[]{:S(2)}) collective-permute-start(bf16[160,1024]{1,0:T(8,128)(2,1)S(1)} %get-tuple-element.135), channel_id=1, source_target_pairs={{64,1},{65,0},{66,3},{67,2},{68,5},{69,4},{70,7},{71,6},{72,9},{73... | collective-permute-start | bytes 983048 | tf_op jit(solution)/shard_map/ppermute | solution.py:64
  127.9 24.0 %collective-permute-start.34 = (bf16[160,1024]{1,0:T(8,128)(2,1)S(1)}, bf16[160,1024]{1,0:T(8,128)(2,1)S(1)}, u32[]{:S(2)}, u32[]{:S(2)}) collective-permute-start(bf16[160,1024]{1,0:T(8,128)(2,1)S(1)} %get-tuple-element.191), channel_id=1, source_target_pairs={{64,1},{65,0},{66,3},{67,2},{68,5},{69,4},{70,7},{71,6},{72,9},{73... | collective-permute-start | bytes 983048 | tf_op jit(solution)/shard_map/ppermute | solution.py:64
  129.2 25.2 %collective-permute-start.18 = (bf16[160,1024]{1,0:T(8,128)(2,1)}, bf16[160,1024]{1,0:T(8,128)(2,1)S(1)}, u32[]{:S(2)}, u32[]{:S(2)}) collective-permute-start(bf16[160,1024]{1,0:T(8,128)(2,1)} %collective-permute-done.17.refs_6_), channel_id=1, source_target_pairs={{0,1},{1,0},{2,3},{3,2},{4,5},{5,4},{6,7},{7,6},{8,9},{9,8},{10,11... | collective-permute-start | bytes 983048 | tf_op jit(solution)/shard_map/ppermute | solution.py:64
  133.0 24.8 %collective-permute-start.24 = (bf16[160,1024]{1,0:T(8,128)(2,1)}, bf16[160,1024]{1,0:T(8,128)(2,1)S(1)}, u32[]{:S(2)}, u32[]{:S(2)}) collective-permute-start(bf16[160,1024]{1,0:T(8,128)(2,1)} %collective-permute-done.17.refs_6_), channel_id=1, source_target_pairs={{0,2},{2,0},{4,6},{6,4},{8,10},{10,8},{12,14},{14,12},{16,18},{18,... | collective-permute-start | bytes 983048 | tf_op jit(solution)/shard_map/ppermute | solution.py:48
  160.1 45.4 %collective-permute-start.39 = (bf16[160,1024]{1,0:T(8,128)(2,1)S(1)}, bf16[160,1024]{1,0:T(8,128)(2,1)S(1)}, u32[]{:S(2)}, u32[]{:S(2)}) collective-permute-start(bf16[160,1024]{1,0:T(8,128)(2,1)S(1)} %collective-permute-done.36.refs_14_), channel_id=1, source_target_pairs={{0,2},{2,0},{4,6},{6,4},{8,10},{10,8},{12,14},{14,12},{16,18},{18,... | collective-permute-start | bytes 983048 | tf_op jit(solution)/shard_map/ppermute | solution.py:48
  164.5 41.0 %collective-permute-start.41 = (bf16[160,1024]{1,0:T(8,128)(2,1)S(1)}, bf16[160,1024]{1,0:T(8,128)(2,1)S(1)}, u32[]{:S(2)}, u32[]{:S(2)}) collective-permute-start(bf16[160,1024]{1,0:T(8,128)(2,1)S(1)} %collective-permute-done.34.refs_6_), channel_id=1, source_target_pairs={{0,2},{2,0},{4,6},{6,4},{8,10},{10,8},{12,14},{14,12},{16,18},{18,... | collective-permute-start | bytes 983048 | tf_op jit(solution)/shard_map/ppermute | solution.py:48
  168.7 36.9 %collective-permute-start.38 = (bf16[160,1024]{1,0:T(8,128)(2,1)S(1)}, bf16[160,1024]{1,0:T(8,128)(2,1)S(1)}, u32[]{:S(2)}, u32[]{:S(2)}) collective-permute-start(bf16[160,1024]{1,0:T(8,128)(2,1)S(1)} %collective-permute-done.37.refs_13_), channel_id=1, source_target_pairs={{0,2},{2,0},{4,6},{6,4},{8,10},{10,8},{12,14},{14,12},{16,18},{18,... | collective-permute-start | bytes 983048 | tf_op jit(solution)/shard_map/ppermute | solution.py:48
  168.7 36.9 %collective-permute-start.40 = (bf16[160,1024]{1,0:T(8,128)(2,1)S(1)}, bf16[160,1024]{1,0:T(8,128)(2,1)S(1)}, u32[]{:S(2)}, u32[]{:S(2)}) collective-permute-start(bf16[160,1024]{1,0:T(8,128)(2,1)S(1)} %collective-permute-done.35.refs_5_), channel_id=1, source_target_pairs={{0,2},{2,0},{4,6},{6,4},{8,10},{10,8},{12,14},{14,12},{16,18},{18,... | collective-permute-start | bytes 983048 | tf_op jit(solution)/shard_map/ppermute | solution.py:48
  246.1 40.7 %collective-permute-start.46 = (f32[80,1280]{1,0:T(8,128)}, f32[80,1280]{1,0:T(8,128)}, u32[]{:S(2)}, u32[]{:S(2)}) collective-permute-start(f32[80,1280]{1,0:T(8,128)} %get-tuple-element.77), channel_id=1, source_target_pairs={{0,4},{2,6},{4,0},{6,2},{8,12},{10,14},{12,8},{14,10},{16,20},{18,... | collective-permute-start | bytes 1228808 | tf_op jit(solution)/shard_map/ppermute | solution.py:48
  247.4 41.6 %collective-permute-start.50 = (f32[80,1280]{1,0:T(8,128)}, f32[80,1280]{1,0:T(8,128)}, u32[]{:S(2)}, u32[]{:S(2)}) collective-permute-start(f32[80,1280]{1,0:T(8,128)} %get-tuple-element.79), channel_id=1, source_target_pairs={{0,12},{2,14},{4,8},{6,10},{8,4},{10,6},{12,0},{14,2},{16,28},{18,... | collective-permute-start | bytes 1228808 | tf_op jit(solution)/shard_map/ppermute | solution.py:48
  252.7 37.6 %collective-permute-start.54 = (f32[80,1280]{1,0:T(8,128)}, f32[80,1280]{1,0:T(8,128)}, u32[]{:S(2)}, u32[]{:S(2)}) collective-permute-start(f32[80,1280]{1,0:T(8,128)} %get-tuple-element.81), channel_id=1, source_target_pairs={{0,16},{2,18},{4,20},{6,22},{8,24},{10,26},{12,28},{14,30},{16,0},... | collective-permute-start | bytes 1228808 | tf_op jit(solution)/shard_map/ppermute | solution.py:48
  262.2 45.5 %collective-permute-start.58 = (f32[80,1920]{1,0:T(8,128)}, f32[80,1920]{1,0:T(8,128)}, u32[]{:S(2)}, u32[]{:S(2)}) collective-permute-start(f32[80,1920]{1,0:T(8,128)} %get-tuple-element.83), channel_id=1, source_target_pairs={{0,48},{2,50},{4,52},{6,54},{8,56},{10,58},{12,60},{14,62},{16,32}... | collective-permute-start | bytes 1843208 | tf_op jit(solution)/shard_map/ppermute | solution.py:48
  286.8 22.2 %collective-permute-start.44 = (bf16[2,160,1024]{2,1,0:T(8,128)(2,1)S(1)}, bf16[2,160,1024]{2,1,0:T(8,128)(2,1)S(1)}, u32[]{:S(2)}, u32[]{:S(2)}) collective-permute-start(bf16[2,160,1024]{2,1,0:T(8,128)(2,1)S(1)} %pad_maximum_fusion.5), channel_id=1, source_target_pairs={{0,2},{2,0},{4,6},{6,4},{8,10},{10,8},{12,14},{14,12},{16,18},{18,... | collective-permute-start | bytes 1966088 | tf_op jit(solution)/shard_map/ppermute | solution.py:48
  289.0 20.3 %collective-permute-start.27 = (bf16[2,160,1024]{2,1,0:T(8,128)(2,1)S(1)}, bf16[2,160,1024]{2,1,0:T(8,128)(2,1)S(1)}, u32[]{:S(2)}, u32[]{:S(2)}) collective-permute-start(bf16[2,160,1024]{2,1,0:T(8,128)(2,1)S(1)} %pad_maximum_fusion.4), channel_id=1, source_target_pairs={{0,2},{2,0},{4,6},{6,4},{8,10},{10,8},{12,14},{14,12},{16,18},{18,... | collective-permute-start | bytes 1966088 | tf_op jit(solution)/shard_map/ppermute | solution.py:48
  309.3 24.2 %collective-permute-start.45 = (bf16[2,2,160,512]{3,2,0,1:T(8,128)(2,1)S(1)}, bf16[2,2,160,512]{3,2,0,1:T(8,128)(2,1)S(1)}, u32[]{:S(2)}, u32[]{:S(2)}) collective-permute-start(bf16[2,2,160,512]{3,2,0,1:T(8,128)(2,1)S(1)} %get-tuple-element.125), channel_id=1, source_target_pairs={{0,1},{1,0},{2,3},{3,2},{4,5},{5,4},{6,7},{7,6},{8,9},{9,8},{10,11... | collective-permute-start | bytes 1966088 | tf_op jit(solution)/shard_map/ppermute | solution.py:60
  310.9 30.3 %collective-permute-start.28 = (bf16[2,2,160,512]{3,2,0,1:T(8,128)(2,1)}, bf16[2,2,160,512]{3,2,0,1:T(8,128)(2,1)}, u32[]{:S(2)}, u32[]{:S(2)}) collective-permute-start(bf16[2,2,160,512]{3,2,0,1:T(8,128)(2,1)} %get-tuple-element.123), channel_id=1, source_target_pairs={{0,1},{1,0},{2,3},{3,2},{4,5},{5,4},{6,7},{7,6},{8,9},{9,8},{10,11... | collective-permute-start | bytes 1966088 | tf_op jit(solution)/shard_map/ppermute | solution.py:60
  (94 other events, 946.7 us)
